TPU v7x, 512 devices: a whole 4x4x16 slice. The times are simulated.
512 devices in a mesh: shard: 32 (over x, y, core), slot: 16 (over z).
Axes of the slice: x: 4, y: 4, z: 16, core: 2. Of those that a mesh axis runs over, the one named last changes fastest.
Arguments:
- embeddings: bfloat16 [131072, 768], P(('shard', 'slot')), may hold values from -8 to 8
- cluster_ids: int32 [131072], P(('shard', 'slot')), may hold values from 0 to 63, as said below
- order_keys: int32 [131072], P(('shard', 'slot')), may hold values from 0 to 131071, each once
Outputs:
- max_similarity: float32 [131072], P(('shard', 'slot'))
Inputs may be any that keep to these rules, and one draw needn't show every extreme that they name: `cluster_ids`: the owner of cluster c is c // 2. Among the 256 rows of one device, at most 8 rows belong to one cluster, and in every device's rows some cluster has exactly 8.
All inputs are finite; a program needn't handle non-finite values.
Results may differ from a plain program's by a relative error of at most 0.00059.
Values may be sent and summed in bfloat16 or wider, within the bound.
A program may use at most 64 MiB of HBM per device.

v0:
```python
import math

import jax
import jax.numpy as jnp
from jax import lax
from jax.sharding import PartitionSpec as P

CL_DEV = 2


def unit_rows(values):
    wide = values.astype(jnp.float32)
    return (wide * lax.rsqrt(jnp.sum(wide * wide, axis=1, keepdims=True) + 1e-06)).astype(
        jnp.bfloat16
    )


def gram(left, right):
    return lax.dot_general(
        left, right, (((1,), (1,)), ((), ())), preferred_element_type=jnp.float32
    )


def local(embeddings, cluster_ids, order_keys):
    unit = unit_rows(embeddings)
    rows_here = embeddings.shape[0]
    width = embeddings.shape[1]
    owners_count = lax.axis_size("shard")
    cluster_count = owners_count * CL_DEV
    capacity = 2 * rows_here // cluster_count
    total = cluster_count * capacity
    onehot = (cluster_ids[:, None] == jnp.arange(cluster_count, dtype=jnp.int32)[None, :]).astype(
        jnp.int32
    )
    position = jnp.sum(jnp.cumsum(onehot, axis=0) * onehot, axis=1) - 1
    target = cluster_ids * capacity + position
    send_rows = jnp.zeros((total, width), jnp.bfloat16).at[target].set(unit)
    send_cl = jnp.full((total,), -1, jnp.int32).at[target].set(cluster_ids)
    send_rank = jnp.zeros((total,), jnp.int32).at[target].set(order_keys)
    held_rows, held_cl, held_rank = (
        lax.all_to_all(send_rows, "shard", split_axis=0, concat_axis=0, tiled=True),
        lax.all_to_all(send_cl, "shard", split_axis=0, concat_axis=0, tiled=True),
        lax.all_to_all(send_rank, "shard", split_axis=0, concat_axis=0, tiled=True),
    )
    start_best = jnp.full((total,), -1.0, jnp.float32)
    best = start_best
    key_rows = lax.all_gather(held_rows, "slot", axis=0, tiled=True)
    key_cl = lax.all_gather(held_cl, "slot", axis=0, tiled=True)
    key_rank = lax.all_gather(held_rank, "slot", axis=0, tiled=True)
    count = key_rows.shape[0]
    step = math.gcd(count, total)
    blocks = count // step

    def one_block(current, items):
        rows, clusters, ranks = items
        sims = gram(held_rows, rows)
        mask = (
            (held_cl[:, None] == clusters[None, :])
            & (clusters[None, :] >= 0)
            & (ranks[None, :] < held_rank[:, None])
        )
        return (jnp.maximum(current, jnp.max(jnp.where(mask, sims, -1.0), axis=1)), None)

    best, unused = lax.scan(
        one_block,
        best,
        (
            key_rows.reshape(blocks, step, width),
            key_cl.reshape(blocks, step),
            key_rank.reshape(blocks, step),
        ),
    )
    returned = lax.all_to_all(best, "shard", split_axis=0, concat_axis=0, tiled=True)
    return returned[target]


def solution(mesh):
    placed = (P(("shard", "slot"), None), P(("shard", "slot")), P(("shard", "slot")))
    return jax.shard_map(
        local, mesh=mesh, in_specs=placed, out_specs=P(("shard", "slot")), check_vma=False
    )
```

profile of v0, /device:TPU:1, one launch (start us, length us, event | category | flops | bytes accessed | tf_op | source)
XLA Modules:
  0.0 245.4 jit_solution(8359553794661072794)
XLA Ops:
  8.1 0.8 fusion.12
  9.5 1.2 fusion.5
  10.7 2.4 scatter_custom_fusion.2
  13.1 24.5 %all_to_all.48 = bf16[32,16,768]{2,1,0:T(8,128)(2,1)} all-to-all(bf16[32,16,768]{2,1,0:T(8,128)(2,1)S(1)} %bitcast.57), channel_id=1, replica_groups=mesh['shard'=32,'slot'=16] {'shard'}, dimensions={0} | all-to-all | bytes 1572864 | tf_op jit(solution)/shard_map/all_to_all | solution.py:41
  37.7 1.6 scatter_custom_fusion
  39.9 3.8 %all-to-all-start = ((s32[32,16,1]{1,2,0:T(1,128)}), s32[32,16,1]{1,2,0:T(1,128)S(1)}, u32[]{:S(2)}, u32[]{:S(2)}) async-start(s32[32,16,1]{1,2,0:T(1,128)} %bitcast.2), calls=%async_computation | async-start | bytes 32768 | tf_op jit(solution)/shard_map/all_to_all | solution.py:42
  43.7 1.6 scatter_custom_fusion.1
  46.0 4.7 %all-to-all-done = s32[32,16,1]{1,2,0:T(1,128)S(1)} async-done(((s32[32,16,1]{1,2,0:T(1,128)}), s32[32,16,1]{1,2,0:T(1,128)S(1)}, u32[]{:S(2)}, u32[]{:S(2)}) %all-to-all-start) | async-done | bytes 2080 | tf_op jit(solution)/shard_map/all_to_all | solution.py:42
  50.7 4.1 %all-to-all-start.1 = ((s32[32,16,1]{1,2,0:T(1,128)}), s32[32,16,1]{1,2,0:T(1,128)S(1)}, u32[]{:S(2)}, u32[]{:S(2)}) async-start(s32[32,16,1]{1,2,0:T(1,128)} %bitcast.3), calls=%async_computation.1 | async-start | bytes 32768 | tf_op jit(solution)/shard_map/all_to_all | solution.py:43
  54.9 29.9 %all-gather = s32[16,1,512]{2,1,0:T(1,128)S(1)} all-gather(s32[1,1,512]{2,1,0:T(1,128)S(1)} %reshape.81), channel_id=1, replica_groups=mesh['shard'=32,'slot'=16] {'slot'}, dimensions={0}, use_global_device_ids=true | all-gather | bytes 34816 | tf_op jit(solution)/shard_map/all_gather | solution.py:48
  86.6 22.4 %all-gather.1 = s32[16,1,512]{2,1,0:T(1,128)S(1)} all-gather(s32[1,1,512]{2,1,0:T(1,128)S(1)} %reshape.83), channel_id=1, replica_groups=mesh['shard'=32,'slot'=16] {'slot'}, dimensions={0}, use_global_device_ids=true | all-gather | bytes 34816 | tf_op jit(solution)/shard_map/all_gather | solution.py:49
  109.2 76.2 %all-gather.4.cloned.1.call-done = bf16[8192,768]{1,0:T(8,128)(2,1)} async-done(((bf16[512,768]{1,0:T(8,128)(2,1)}), bf16[8192,768]{1,0:T(8,128)(2,1)}) %all-gather.4.cloned.1.call-update) | async-done | bytes 12582928 | tf_op jit(solution)/shard_map/all_gather | solution.py:47
  185.4 34.2 %while.11 = (s32[]{:T(128)}, f32[512]{0:T(512)S(1)}, s32[512]{0:T(512)S(1)}, s32[16,512]{1,0:T(8,128)S(1)}, s32[16,512]{1,0:T(8,128)S(1)}, /*index=5*/s32[512]{0...) while((s32[]{:T(128)}, f32[512]{0:T(512)S(1)}, ...), condition=%wide.region_9.10_spmd.clone, body=%wide.region_7.9_spmd.clone.sunk | while | flops 404227072 | bytes 1598595 | solution.py:64
  185.4 2.1 fusion.24
  187.5 2.1 fusion.24
  189.7 2.1 fusion.24
  191.8 2.1 fusion.24
  193.9 2.1 fusion.24
  196.1 2.1 fusion.24
  198.2 2.1 fusion.24
  200.4 2.1 fusion.24
  202.5 2.1 fusion.24
  204.7 2.1 fusion.24
  206.8 2.1 fusion.24
  208.9 2.1 fusion.24
  211.1 2.1 fusion.24
  213.2 2.1 fusion.24
  215.4 2.1 fusion.24
  217.5 2.1 fusion.24
  220.3 7.5 %all-to-all-start.3 = ((f32[32,16,1]{1,2,0:T(1,128)}), f32[32,16,1]{1,2,0:T(1,128)S(1)}, u32[]{:S(2)}, u32[]{:S(2)}) async-start(f32[32,16,1]{1,2,0:T(1,128)} %bitcast.7), calls=%async_computation.3 | async-start | bytes 32768 | tf_op jit(solution)/shard_map/all_to_all | solution.py:73
  227.8 6.9 %all-to-all-done.3 = f32[32,16,1]{1,2,0:T(1,128)S(1)} async-done(((f32[32,16,1]{1,2,0:T(1,128)}), f32[32,16,1]{1,2,0:T(1,128)S(1)}, u32[]{:S(2)}, u32[]{:S(2)}) %all-to-all-start.3) | async-done | bytes 2080 | tf_op jit(solution)/shard_map/all_to_all | solution.py:73
  236.0 2.5 %gather_fusion = f32[256]{0:T(256)} fusion(f32[512]{0:T(512)S(1)} %all_to_all.43, s32[1024]{0:T(1024)S(1)} %pad_clamp_fusion), kind=kCustom, calls=%fused_computation | custom fusion | bytes 3072 | tf_op jit(solution)/shard_map/gather | solution.py:74
  (75 shorter events, 8.4 us)
Async XLA Ops:
  6.5 178.8 %all-gather.4.cloned.1.call-start = ((), (), s32[]{:S(2)}) async-start(), calls=%async_computation.4 | async-start | bytes 13369344 | tf_op jit(solution)/shard_map/all_gather | solution.py:47
  39.9 10.7 %all-to-all-start = ((s32[32,16,1]{1,2,0:T(1,128)}), s32[32,16,1]{1,2,0:T(1,128)S(1)}, u32[]{:S(2)}, u32[]{:S(2)}) async-start(s32[32,16,1]{1,2,0:T(1,128)} %bitcast.2), calls=%async_computation | async-start | bytes 32768 | tf_op jit(solution)/shard_map/all_to_all | solution.py:42
  50.7 35.3 %all-to-all-start.1 = ((s32[32,16,1]{1,2,0:T(1,128)}), s32[32,16,1]{1,2,0:T(1,128)S(1)}, u32[]{:S(2)}, u32[]{:S(2)}) async-start(s32[32,16,1]{1,2,0:T(1,128)} %bitcast.3), calls=%async_computation.1 | async-start | bytes 32768 | tf_op jit(solution)/shard_map/all_to_all | solution.py:43
  220.3 14.5 %all-to-all-start.3 = ((f32[32,16,1]{1,2,0:T(1,128)}), f32[32,16,1]{1,2,0:T(1,128)S(1)}, u32[]{:S(2)}, u32[]{:S(2)}) async-start(f32[32,16,1]{1,2,0:T(1,128)} %bitcast.7), calls=%async_computation.3 | async-start | bytes 32768 | tf_op jit(solution)/shard_map/all_to_all | solution.py:73
Sparse Core Ops, SparseCore 0:
  37.8 147.4 all-gather.3
where the time goes:
time: 246 us; the launch traced here: 245 us
  waiting for transfers between devices  87.8 us (36%)
  blocking collectives  76.8 us (31%)
  matrix products  32.9 us (13%)
  starting transfers between devices  15.5 us (6%)
  between operations  13.5 us (5%)
  local copies, waits for them, and re-layouts  9.41 us (4%)
  other arithmetic  8.96 us (4%)
    all_gather x1, waiting for transfers between devices, local(): key_rows = lax.all_gather(held_rows, 'slot', axis=0, tiled=True)  76.2 us
    dot_general x16, matrix products, gram(): lax.dot_general(left, right, (((1,), (1,)), ((), ())), preferred_element_...  32.9 us
    all_gather x1, blocking collectives, local(): key_cl = lax.all_gather(held_cl, 'slot', axis=0, tiled=True)  29.9 us
    all_to_all x1, blocking collectives, local(): lax.all_to_all(send_rows, 'shard', split_axis=0, concat_axis=0, tiled=True)  24.5 us
    all_gather x1, blocking collectives, local(): key_rank = lax.all_gather(held_rank, 'slot', axis=0, tiled=True)  22.4 us
    all_to_all x1, starting transfers between devices, local(): lax.all_to_all(best, 'shard', split_axis=0, concat_axis=0, tiled=True)  7.54 us
    all_to_all x1, waiting for transfers between devices, local(): lax.all_to_all(best, 'shard', split_axis=0, concat_axis=0, tiled=True)  6.93 us
  transfers between devices with their start and end apart: 4, of which 3 were waited for; matrix products, arithmetic and copies ran while one was open for 2% of the time, Pallas kernels for 0%

commit v1 on v0

v1 whole, which is shorter than its diff:
```python
import jax
import jax.numpy as jnp
from jax import lax
from jax.experimental import pallas as pl
from jax.experimental.pallas import tpu as pltpu
from jax.sharding import PartitionSpec as P

MESH = pl.DeviceIdType.MESH
F32, BF16 = jnp.float32, jnp.bfloat16
NX, NY, NZ = 4, 4, 16
CAP = 8
PER = 16
CHUNKS = NY * NZ // PER
LANES = PER * CAP
BLOCKS = NY * NZ
NEVER = 1e9
A1, A0, R0, R1, L0 = range(5)


def iota(shape, axis):
    return lax.broadcasted_iota(jnp.int32, shape, axis)


def kernel(x_ref, ids_ref, keys_ref, out_ref, place, sent, sent_rank, got, got_rank, rows, ranks, keyed, best, part, other,
           final, back, z_send, z_recv, zr_send, zr_recv, x_send, x_recv, xr_send, xr_recv, p_send, p_recv, b_send, b_recv):
    shard, z = lax.axis_index("shard"), lax.axis_index("slot")
    x, y, core = shard // 8, (shard // 2) % 4, shard % 2

    def at(x_, y_, core_, z_):
        return ((x_ * NY + y_) * 2 + core_, z_)

    def home(r):
        return at(x, (y + r // NZ) % NY, core, (z + r % NZ) % NZ)

    def source(r):
        return at(x, (y + NY - r // NZ) % NY, core, (z + NZ - r % NZ) % NZ)

    right, left = (x + 1) % NX, (x + NX - 1) % NX
    twin = at(x, y, 1 - core, z)
    to_right, to_left = at(right, y, core, z), at(left, y, core, z)
    to_cross, from_cross = at(right, y, 1 - core, z), at(left, y, 1 - core, z)

    barrier = pltpu.get_barrier_semaphore()

    def greet(r, carry):
        pl.semaphore_signal(barrier, inc=1, device_id=source(r), device_id_type=MESH)
        return carry

    lax.fori_loop(1, BLOCKS, greet, 0)
    for device in (twin, to_right, to_left, from_cross):
        pl.semaphore_signal(barrier, inc=1, device_id=device, device_id_type=MESH)

    ids = ids_ref[...]
    idf = ids.astype(F32)
    across = jnp.broadcast_to(idf, (256, 256))
    down = jnp.transpose(across)
    before = (across == down) & (iota((256, 256), 0) < iota((256, 256), 1))
    position = jnp.sum(jnp.where(before, 1.0, 0.0), axis=0, keepdims=True).astype(jnp.int32)
    step_y, step_z = ((ids & 3) + NY - y) & (NY - 1), ((ids >> 2) + NZ - z) & (NZ - 1)
    target = (step_y * NZ + step_z) * CAP + position
    place[...] = jnp.where(iota((BLOCKS * CAP, 256), 0) == target, 1.0, 0.0).astype(BF16)

    wide = x_ref[...].astype(F32)
    unit = (wide * lax.rsqrt(jnp.sum(wide * wide, axis=1, keepdims=True) + 1e-6)).astype(BF16)
    for g in range(CHUNKS):
        laid = jnp.dot(place[g * LANES:(g + 1) * LANES, :], unit, preferred_element_type=F32)
        low = laid[:, :384].reshape(PER, CAP, 384)
        high = laid[:, 384:].reshape(PER, CAP, 384)
        sent[g * PER:(g + 1) * PER] = jnp.concatenate([low, high], axis=1).astype(BF16)

    value = keys_ref[...] + 1
    upper = (value + 256) >> 9
    lower = value - upper * 512
    digits = jnp.where(iota((16, 256), 0) == 0, upper, jnp.where(iota((16, 256), 0) == 1, lower, 0))
    found = lax.dot_general(digits.astype(F32).astype(BF16), place[...], (((1,), (1,)), ((), ())), preferred_element_type=F32)
    value = found[0:1] * 512.0 + found[1:2]
    for g in range(CHUNKS):
        sent_rank[g] = value[:, g * LANES:(g + 1) * LANES]

    pl.semaphore_wait(barrier, BLOCKS - 1 + 4)

    def scatter(r, carry):
        g = r // PER
        pltpu.make_async_remote_copy(src_ref=sent_rank.at[g], dst_ref=got_rank.at[r], send_sem=zr_send, recv_sem=zr_recv.at[g],
                                     device_id=home(r), device_id_type=MESH).start()
        pltpu.make_async_remote_copy(src_ref=sent.at[r], dst_ref=got.at[r], send_sem=z_send, recv_sem=z_recv.at[g],
                                     device_id=home(r), device_id_type=MESH).start()
        return carry

    lax.fori_loop(1, BLOCKS, scatter, 0)
    got[0] = sent[0]
    got_rank[0] = sent_rank[0]
    best[...] = jnp.full(best.shape, -1.0, F32)

    mine = iota((PER, LANES), 1) // CAP == iota((PER, LANES), 0)

    def pass_on(g, a, b, device):
        sends = []
        for i, (ref, send, recv) in enumerate(((rows, x_send, x_recv), (ranks, xr_send, xr_recv))):
            copy = pltpu.make_async_remote_copy(src_ref=ref.at[g, a], dst_ref=ref.at[g, b], send_sem=send.at[g, b], recv_sem=recv.at[g, b],
                                                device_id=device, device_id_type=MESH)
            copy.start()
            sends.append(copy)
        return sends

    def key_side(g, a):
        rank = ranks[g, a]
        rank = jnp.where(rank > 0.5, rank, NEVER)
        keyed[g, a] = jnp.transpose(jnp.broadcast_to(rank, (LANES, LANES)))

    def fold(sims, g, a, h, q):
        masked = jnp.where(keyed[g, a] < ranks[h, q], sims, -1.0)
        best[h, q] = jnp.maximum(best[h, q], jnp.max(masked.reshape(LANES // 8, 8, LANES), axis=0))

    def dots(k, q):
        return lax.dot_general(k, q, (((1,), (1,)), ((), ())), preferred_element_type=F32)

    def inner(g, h):
        sims = dots(rows[g, A0:R1].reshape(2 * LANES, 768), rows[h, A1:R0].reshape(2 * LANES, 768))
        for i, a in enumerate((A0, R0)):
            for j, q in enumerate((A1, A0)):
                fold(sims[i * LANES:(i + 1) * LANES, j * LANES:(j + 1) * LANES], g, a, h, q)

    def outer(g, h):
        sims = dots(rows[g, L0], rows[h, A1:L0].reshape(4 * LANES, 768))
        for j, q in enumerate((A1, A0, R0, R1)):
            fold(sims[:, j * LANES:(j + 1) * LANES], g, L0, h, q)

    def pairs(g, work):
        def one(h, carry):
            work(h, g)
            work(g, h)
            return carry

        lax.fori_loop(0, g, one, 0)
        work(g, g)

    copies = []
    for g in range(CHUNKS):
        first = 1 if g == 0 else 0
        blocks = got.at[pl.ds(g * PER + first, PER - first)]
        pltpu.make_async_copy(blocks, blocks, z_recv.at[g]).wait()
        lanes = got_rank.at[pl.ds(g * PER + first, PER - first)]
        pltpu.make_async_copy(lanes, lanes, zr_recv.at[g]).wait()
        block = got[g * PER:(g + 1) * PER].astype(F32)
        rows[g, A0] = jnp.concatenate([block[:, :CAP].reshape(LANES, 384), block[:, CAP:].reshape(LANES, 384)], axis=1).astype(BF16)
        lane = got_rank[g * PER:(g + 1) * PER].reshape(PER, LANES)
        ranks[g, A0] = jnp.sum(jnp.where(mine, lane, 0.0), axis=0, keepdims=True)
        to_l, to_r, to_t = pass_on(g, A0, R0, to_left), pass_on(g, A0, L0, to_right), pass_on(g, A0, A1, twin)
        key_side(g, A0)
        for copy in to_l:
            copy.wait_recv()
        to_t2 = pass_on(g, R0, R1, twin)
        key_side(g, R0)
        for copy in to_t:
            copy.wait_recv()
        pairs(g, inner)
        for copy in to_r:
            copy.wait_recv()
        key_side(g, L0)
        for copy in to_t2:
            copy.wait_recv()
        pairs(g, outer)
        copies += to_l + to_r + to_t + to_t2

    for g in range(CHUNKS):
        for q in range(4):
            part[q, g] = jnp.max(best[g, q], axis=0, keepdims=True)
    shares = [
        pltpu.make_async_remote_copy(src_ref=part.at[q], dst_ref=other.at[i], send_sem=p_send.at[i], recv_sem=p_recv.at[i],
                                     device_id=device, device_id_type=MESH)
        for i, (q, device) in enumerate(((A1, twin), (R0, to_right), (R1, to_cross)))
    ]
    for copy in shares:
        copy.start()
    for copy in shares:
        copy.wait_recv()
    final[...] = jnp.maximum(jnp.maximum(part[A0], other[0]), jnp.maximum(other[1], other[2]))

    def give(r, carry):
        pltpu.make_async_remote_copy(src_ref=final.at[r // PER], dst_ref=back.at[r], send_sem=b_send, recv_sem=b_recv,
                                     device_id=source(r), device_id_type=MESH).start()
        return carry

    lax.fori_loop(1, BLOCKS, give, 0)
    back[0] = final[0]
    for copy in copies + shares:
        copy.wait_send()
    blocks = sent.at[pl.ds(1, BLOCKS - 1)]
    pltpu.make_async_copy(blocks, blocks, z_send).wait()
    lanes = got_rank.at[pl.ds(1, BLOCKS - 1)]
    pltpu.make_async_copy(lanes, lanes, zr_send).wait()
    lanes = back.at[pl.ds(1, BLOCKS - 1)]
    pltpu.make_async_copy(lanes, lanes, b_recv).wait()
    total = jnp.zeros((1, 256), F32)
    for g in range(CHUNKS):
        lane = back[g * PER:(g + 1) * PER].reshape(PER, LANES)
        held = jnp.sum(jnp.where(mine, lane, 0.0), axis=0, keepdims=True)
        one = held.astype(BF16).astype(F32)
        two = (held - one).astype(BF16).astype(F32)
        three = held - one - two
        row = iota((16, LANES), 0)
        split = jnp.where(row == 0, one, jnp.where(row == 1, two, jnp.where(row == 2, three, 0.0))).astype(BF16)
        picked = jnp.dot(split, place[g * LANES:(g + 1) * LANES, :], preferred_element_type=F32)
        total = total + (picked[0:1] + picked[1:2] + picked[2:3])
    out_ref[...] = total
    pltpu.make_async_copy(lanes, lanes, b_send).wait()


def local(embeddings, cluster_ids, order_keys):
    dma = pltpu.SemaphoreType.DMA
    vmem = pl.BlockSpec(memory_space=pltpu.VMEM)
    out = pl.pallas_call(
        kernel,
        out_shape=jax.ShapeDtypeStruct((1, 256), F32),
        in_specs=[vmem, vmem, vmem],
        out_specs=vmem,
        scratch_shapes=[
            pltpu.VMEM((BLOCKS * CAP, 256), BF16),
            pltpu.VMEM((BLOCKS, 16, 384), BF16),
            pltpu.VMEM((CHUNKS, 1, LANES), F32),
            pltpu.VMEM((BLOCKS, 16, 384), BF16),
            pltpu.VMEM((BLOCKS, 1, LANES), F32),
            pltpu.VMEM((CHUNKS, 5, LANES, 768), BF16),
            pltpu.VMEM((CHUNKS, 5, 1, LANES), F32),
            pltpu.VMEM((CHUNKS, 5, LANES, LANES), F32),
            pltpu.VMEM((CHUNKS, 4, 8, LANES), F32),
            pltpu.VMEM((4, CHUNKS, 1, LANES), F32),
            pltpu.VMEM((3, CHUNKS, 1, LANES), F32),
            pltpu.VMEM((CHUNKS, 1, LANES), F32),
            pltpu.VMEM((BLOCKS, 1, LANES), F32),
            dma, dma((CHUNKS,)), dma, dma((CHUNKS,)),
            dma((CHUNKS, 5)), dma((CHUNKS, 5)), dma((CHUNKS, 5)), dma((CHUNKS, 5)),
            dma((3,)), dma((3,)), dma, dma,
        ],
        compiler_params=pltpu.CompilerParams(collective_id=0, has_side_effects=True, vmem_limit_bytes=40 * 2**20),
    )(embeddings, cluster_ids.reshape(1, 256), order_keys.reshape(1, 256))
    return out.reshape(256)


def solution(mesh):
    placed = (P(("shard", "slot"), None), P(("shard", "slot")), P(("shard", "slot")))
    return jax.shard_map(local, mesh=mesh, in_specs=placed, out_specs=P(("shard", "slot")), check_vma=False)
```

time: 246 us -> 87.9 us (0.36)
  waiting for transfers between devices: 87.8 us -> 0 us
  Pallas kernels: 0 us -> 85.5 us
  blocking collectives: 76.8 us -> 0 us
  matrix products: 32.9 us -> 0 us
  starting transfers between devices: 15.5 us -> 0 us
  between operations: 13.5 us -> 0.01 us
  other arithmetic: 8.96 us -> 0 us
  local copies, waits for them, and re-layouts: 9.41 us -> 2.25 us
    pallas_call x0 -> x1, Pallas kernels: none -> 85.5 us  [local(): pl.pallas_call(kernel, out_shape=jax.ShapeDtypeStruct((1, 256), F32), in_...]
    all_gather x1 -> x0, waiting for transfers between devices: 76.2 us -> none  [local(): key_rows = lax.all_gather(held_rows, 'slot', axis=0, tiled=True)]
    all_gather x2 -> x0, blocking collectives: 52.3 us -> none  [the longest x1 29.9 us: local(): key_cl = lax.all_gather(held_cl, 'slot', axis=0, tiled=True)]
    dot_general x16 -> x0, matrix products: 32.9 us -> none  [gram(): lax.dot_general(left, right, (((1,), (1,)), ((), ())), preferred_element_...]
    all_to_all x1 -> x0, blocking collectives: 24.5 us -> none  [local(): lax.all_to_all(send_rows, 'shard', split_axis=0, concat_axis=0, tiled=True)]
    all_to_all x3 -> x0, starting transfers between devices: 15.5 us -> none  [the longest x1 7.54 us: local(): lax.all_to_all(best, 'shard', split_axis=0, concat_axis=0, tiled=True)]
    all_to_all x3 -> x0, waiting for transfers between devices: 11.6 us -> none  [the longest x1 6.93 us: local(): lax.all_to_all(best, 'shard', split_axis=0, concat_axis=0, tiled=True)]
    all_to_all x8 -> x0, local copies, waits for them, and re-layouts: 3.29 us -> none  [the longest x3 1.27 us: local(): lax.all_to_all(best, 'shard', split_axis=0, concat_axis=0, tiled=True)]
  transfers between devices with their start and end apart: 4 -> 0, of which waited for: 3 -> 0; matrix products, arithmetic and copies ran while one was open for 2% -> 0% of each run, Pallas kernels for 0% -> 0%
where the time goes in v1:
time: 87.9 us; the launch traced here: 87.8 us
  Pallas kernels  85.5 us (97%)
  local copies, waits for them, and re-layouts  2.25 us (3%)
    pallas_call x1, Pallas kernels, local(): pl.pallas_call(kernel, out_shape=jax.ShapeDtypeStruct((1, 256), F32), in_...  85.5 us
    unnamed x7, local copies, waits for them, and re-layouts  2.25 us

profile of v1, /device:TPU:1, one launch (start us, length us, event | category | flops | bytes accessed | tf_op | source)
XLA Modules:
  0.0 87.8 jit_solution(3509896427915568655)
XLA Ops:
  0.0 0.0 copy-start.2
  0.0 0.0 copy-start.1
  0.0 0.7 copy-done.2
  0.7 0.0 copy-done.1
  0.7 0.0 copy-start
  0.7 1.0 %copy-done = bf16[256,768]{1,0:T(8,128)(2,1)S(1)} copy-done((bf16[256,768]{1,0:T(8,128)(2,1)S(1)}, bf16[256,768]{1,0:T(8,128)(2,1)}, u32[]{:S(2)}) %copy-start) | copy-done | bytes 393240
  1.7 85.5 %shard_map.37 = f32[1,256]{1,0:T(1,128)S(1)} custom-call(bf16[256,768]{1,0:T(8,128)(2,1)S(1)} %copy-done, s32[1,256]{1,0:T(1,128)S(1)} %bitcast.4, s32[1,256]{1,0:T(1,128)S(1)} %bitcast.5), custom_call_target="tpu_custom_call" | custom-call | tf_op jit(solution)/shard_map/pallas_call | solution.py:213
  87.2 0.6 copy.5
Async XLA Ops:
  0.0 0.7 copy-start.2
  0.0 0.7 copy-start.1
  0.7 1.0 %copy-start = (bf16[256,768]{1,0:T(8,128)(2,1)S(1)}, bf16[256,768]{1,0:T(8,128)(2,1)}, u32[]{:S(2)}) copy-start(bf16[256,768]{1,0:T(8,128)(2,1)} %x_ref.1) | copy-start | bytes 1179652

commit v2 on v0

v2 whole, which is shorter than its diff:
```python
import jax
import jax.numpy as jnp
from jax import lax
from jax.experimental import pallas as pl
from jax.experimental.pallas import tpu as pltpu
from jax.sharding import PartitionSpec as P

MESH = pl.DeviceIdType.MESH
F32, BF16 = jnp.float32, jnp.bfloat16
NX, NY, NZ = 4, 4, 16
D, CAP = 768, 8
ROWS = 256
BIG, SMALL = 128, 64
SUB = 4
SUBS = NZ // SUB
PLACES = SUB * CAP
LAG = 2
NEVER = 1e9
ORDER = (0, 1, 3, 2)
A1, A0, R0, R1, L0 = range(5)


def iota(shape, axis):
    return lax.broadcasted_iota(jnp.int32, shape, axis)


def way(b):
    return 8 + b // 2 - (b % 2) * (1 + 2 * (b // 2))


def turn(rows):
    group = iota((1, 128), 1) // 32
    out = []
    for j in range(4):
        row = rows[0] if j == 0 else pltpu.roll(rows[0], (32 * (0 - j)) % 128, 1)
        for i in range(1, 4):
            shift = (32 * (i - j)) % 128
            row = jnp.where(group == i, rows[i] if shift == 0 else pltpu.roll(rows[i], shift, 1), row)
        out.append(row)
    return out


def collect(ref):
    held = ref[...].reshape(NZ, 128)
    held = jnp.where((iota((NZ, 128), 1) // CAP) % 4 == iota((NZ, 128), 0) % 4, held, 0.0)
    return turn([jnp.sum(held[4 * q:4 * q + 4], axis=0, keepdims=True) for q in range(4)])


def kernel(x_hbm, ids_hbm, keys_hbm, out_ref, x_ref, ids_ref, keys_ref, place, sent, stage, got, rank_out, rank_mid,
           rank_turned, rank_got, ranks, big, small, keyed, query, best, part, half, whole, other, turned, back,
           in_sem, y_send, y_recv, yr_send, yr_recv, z_send, z_recv, zr_send, zr_recv, x_send, x_recv, xr_send, xr_recv,
           h_send, h_recv, p_send, p_recv, b_send, b_recv):
    shard, z = lax.axis_index("shard"), lax.axis_index("slot")
    x, y, core = shard // 8, (shard // 2) % 4, shard % 2

    def at(dx, dy, flip, dz):
        core_ = 1 - core if flip else core
        return ((((x + dx) % NX) * NY + (y + dy) % NY) * 2 + core_, (z + dz) % NZ)

    twin, right, left = at(0, 0, True, 0), at(1, 0, False, 0), at(3, 0, False, 0)

    def remote(src, dst, send, recv, device):
        return pltpu.make_async_remote_copy(src_ref=src, dst_ref=dst, send_sem=send, recv_sem=recv, device_id=device,
                                            device_id_type=MESH)

    def await_bytes(ref, sem):
        pltpu.make_async_copy(ref, ref, sem).wait()

    loads = [pltpu.make_async_copy(a, b, in_sem.at[i])
             for i, (a, b) in enumerate(((ids_hbm, ids_ref), (keys_hbm, keys_ref), (x_hbm, x_ref)))]
    for load in loads:
        load.start()

    barrier = pltpu.get_barrier_semaphore()

    def greet(device):
        pl.semaphore_signal(barrier, inc=1, device_id=device, device_id_type=MESH)

    def greet_z(d, carry):
        greet(at(0, 0, False, d))
        return carry

    for device in (twin, right):
        greet(device)
    for g in range(NY):
        greet(at(3, g, False, 0))
        if g:
            greet(at(0, g, False, 0))
    lax.fori_loop(1, NZ, greet_z, 0)

    loads[0].wait()
    ids = ids_ref[...]
    across = jnp.broadcast_to(ids.astype(F32), (ROWS, ROWS))
    before = (across == jnp.transpose(across)) & (iota((ROWS, ROWS), 0) < iota((ROWS, ROWS), 1))
    position = jnp.sum(jnp.where(before, 1.0, 0.0), axis=0, keepdims=True).astype(jnp.int32)
    step_y, step_z = ((ids & 3) + NY - y) & (NY - 1), ((ids >> 2) + NZ - z) & (NZ - 1)
    block = jnp.where(step_z < 8, 15 - 2 * step_z, 2 * step_z - 16)
    target = (step_y * NZ + block) * CAP + position
    place[...] = jnp.where(iota((NY * BIG, ROWS), 0) == target, 1.0, 0.0).astype(BF16)

    loads[1].wait()
    value = keys_ref[...] + 1
    upper = (value + 256) >> 9
    lower = value - upper * 512
    digits = jnp.where(iota((16, ROWS), 0) == 0, upper, jnp.where(iota((16, ROWS), 0) == 1, lower, 0))
    found = lax.dot_general(digits.astype(F32).astype(BF16), place[...], (((1,), (1,)), ((), ())), preferred_element_type=F32)
    value = found[0:1] * 512.0 + found[1:2]
    for g in range(NY):
        rank_out[g] = value[:, g * BIG:(g + 1) * BIG]

    loads[2].wait()
    wide = x_ref[...].astype(F32)
    unit = (wide * lax.rsqrt(jnp.sum(wide * wide, axis=1, keepdims=True) + 1e-6)).astype(BF16)
    for g in range(NY):
        laid = jnp.dot(place[g * BIG:(g + 1) * BIG, :], unit, preferred_element_type=F32)
        halves = [laid[:, :D // 2].reshape(NZ, CAP, D // 2), laid[:, D // 2:].reshape(NZ, CAP, D // 2)]
        sent[g] = jnp.concatenate(halves, axis=1).astype(BF16)

    pl.semaphore_wait(barrier, 24)

    def along_z(g, source):
        def go(b, carry):
            remote(source.at[g, b], got.at[g, b], z_send, z_recv.at[g, b // SUB], at(0, 0, False, way(b))).start()
            return carry

        lax.fori_loop(0, NZ - 1, go, 0)
        got[g, NZ - 1] = source[g, NZ - 1]

    for g in ORDER[1:]:
        remote(rank_out.at[g], rank_mid.at[g], yr_send, yr_recv, at(0, g, False, 0)).start()
    along_y = {g: remote(sent.at[g], stage.at[g], y_send.at[g], y_recv.at[g], at(0, g, False, 0)) for g in ORDER[1:]}
    along_y[1].start()
    along_z(0, sent)
    along_y[3].start()
    along_y[2].start()

    best[...] = jnp.full(best.shape, -1.0, F32)
    await_bytes(rank_mid.at[pl.ds(1, NY - 1)], yr_recv)
    for q, row in enumerate(turn([rank_out[0]] + [rank_mid[g] for g in range(1, NY)])):
        rank_turned[q] = row

    def ranks_along_z(b, carry):
        remote(rank_turned.at[b // SUB], rank_got.at[b], zr_send, zr_recv, at(0, 0, False, way(b))).start()
        return carry

    lax.fori_loop(0, NZ - 1, ranks_along_z, 0)
    rank_got[NZ - 1] = rank_turned[SUBS - 1]
    for g in ORDER[1:]:
        along_y[g].wait_recv()
        along_z(g, stage)

    await_bytes(rank_got.at[pl.ds(0, NZ - 1)], zr_recv)
    for g, row in enumerate(collect(rank_got)):
        ranks[A0, g] = row
    shared = [remote(ranks.at[a], ranks.at[b], xr_send.at[i], xr_recv.at[i], device)
              for i, (a, b, device) in enumerate(((A0, R0, left), (A0, L0, right), (A0, A1, twin), (R0, R1, twin)))]
    for copy in shared[:3]:
        copy.start()

    def rows_of(i, sub, a):
        if i < 3:
            return big.at[i, a, pl.ds(sub * PLACES, PLACES)]
        return small.at[sub // 2, a, pl.ds(sub % 2 * PLACES, PLACES)]

    def passed(i, sub, j):
        a, b, device = ((A0, R0, left), (A0, L0, right), (A0, A1, twin), (R0, R1, twin))[j]
        return remote(rows_of(i, sub, a), rows_of(i, sub, b), x_send.at[j], x_recv.at[i * SUBS + sub, j], device)

    def pass_on(i, sub):
        g = ORDER[i]
        first = sub * SUB
        count = SUB - 1 if sub == SUBS - 1 else SUB
        await_bytes(got.at[g, pl.ds(first, count)], z_recv.at[g, sub])
        held = got[g, first:first + SUB].astype(F32)
        rows = jnp.concatenate([held[:, :CAP].reshape(PLACES, D // 2), held[:, CAP:].reshape(PLACES, D // 2)], axis=1)
        rows_of(i, sub, A0)[...] = rows.astype(BF16)
        for j in range(3):
            passed(i, sub, j).start()

    def pass_twin(i, sub):
        passed(i, sub, 0).wait_recv()
        passed(i, sub, 3).start()

    def learn_ranks():
        for copy in shared[:3]:
            copy.wait_recv()
        shared[3].start()
        for i, g in enumerate(ORDER):
            for s, a in enumerate((A0, R0, L0)):
                rank = ranks[a, g]
                rank = jnp.where(rank > 0.5, rank, NEVER)
                keyed[i, s] = jnp.transpose(jnp.broadcast_to(rank, (BIG, BIG)))
        shared[3].wait_recv()
        for i in range(3):
            for a in (A1, A0, R0, R1):
                query[4 * i + a] = ranks[a, ORDER[i]]
        low = iota((1, BIG), 1) < SMALL
        for s, (a, b) in enumerate(((A1, A0), (R0, R1))):
            one, two = ranks[a, ORDER[3]], ranks[b, ORDER[3]]
            query[12 + s] = jnp.where(low, one, pltpu.roll(two, SMALL, 1))
            query[14 + s] = jnp.where(low, pltpu.roll(one, SMALL, 1), two)

    def dots(k, q):
        return lax.dot_general(k, q, (((1,), (1,)), ((), ())), preferred_element_type=F32)

    def rows_in(p, a, b):
        if isinstance(p, int) and p >= 3:
            return small[p - 3, a:b].reshape((b - a) * SMALL, D)
        return big[p, a:b].reshape((b - a) * BIG, D)

    def key_ranks(p, s):
        if isinstance(p, int) and p >= 3:
            return keyed[3, s, (p - 3) * SMALL:(p - 2) * SMALL]
        return keyed[p, s]

    def groups(q, outer):
        if isinstance(q, int) and q >= 3:
            return [12 + 2 * (q - 3) + s for s in range(2 if outer else 1)]
        return [4 * q + a for a in range(4 if outer else 2)]

    def fold(sims, rank, j):
        masked = jnp.where(rank < query[j], sims, -1.0)
        best[j] = jnp.maximum(best[j], jnp.max(masked.reshape(sims.shape[0] // 8, 8, 128), axis=0))

    def inner(k, q):
        sims = dots(rows_in(k, A0, R1), rows_in(q, A1, R0))
        size = sims.shape[0] // 2
        for s in range(2):
            for n, j in enumerate(groups(q, False)):
                fold(sims[s * size:(s + 1) * size, n * 128:(n + 1) * 128], key_ranks(k, s), j)

    def outer(k, q):
        sims = dots(rows_in(k, L0, L0 + 1), rows_in(q, A1, L0))
        for n, j in enumerate(groups(q, True)):
            fold(sims[:, n * 128:(n + 1) * 128], key_ranks(k, 2), j)

    def pairs(p, work):
        def one(h, carry):
            work(h, p)
            work(p, h)
            return carry

        lax.fori_loop(0, min(p, 3), one, 0)
        if p == 4:
            work(3, 4)
            work(4, 3)
        work(p, p)

    def subs_of(p):
        return [(p, sub) for sub in range(SUBS)] if p < 3 else [(3, 2 * (p - 3)), (3, 2 * (p - 3) + 1)]

    def compare_inner(p):
        for i, sub in subs_of(p):
            passed(i, sub, 2).wait_recv()
        pairs(p, inner)

    def compare_outer(p):
        for i, sub in subs_of(p):
            passed(i, sub, 1).wait_recv()
            passed(i, sub, 3).wait_recv()
        pairs(p, outer)

    for n in range(4 * SUBS):
        pass_on(n // SUBS, n % SUBS)
        if n == 0:
            learn_ranks()
        if n >= LAG:
            pass_twin((n - LAG) // SUBS, (n - LAG) % SUBS)
        i, sub = divmod(n - LAG, SUBS)
        if sub == SUBS - 1 and 0 <= i < 3:
            compare_inner(i)
        if sub == 0 and 0 < i < 4:
            compare_outer(i - 1)
    compare_inner(3)
    compare_outer(3)
    for n in range(4 * SUBS - LAG, 4 * SUBS):
        pass_twin(n // SUBS, n % SUBS)
    compare_inner(4)
    compare_outer(4)

    low = iota((1, BIG), 1) < SMALL
    top = [jnp.max(best[j], axis=0, keepdims=True) for j in range(16)]
    for a in (A1, A0, R0, R1):
        for i in range(3):
            part[a, ORDER[i]] = top[4 * i + a]
        one, two = top[12 + a // 2], top[14 + a // 2]
        part[a, ORDER[3]] = (jnp.where(low, one, pltpu.roll(two, SMALL, 1)) if a in (A1, R0) else
                             jnp.where(low, pltpu.roll(one, SMALL, 1), two))
    halves = [remote(part.at[a], half.at[i], h_send.at[i], h_recv.at[i], twin) for i, a in enumerate((R1, A1))]
    for copy in halves:
        copy.start()
    for n, (a, dx) in enumerate(((R0, 1), (A0, 0))):
        halves[n].wait_recv()
        for g in (2, 1, 3, 0):
            whole[n, g] = jnp.maximum(part[a, g], half[n, g])
            if dx or g:
                remote(whole.at[n, g], other.at[n, g], p_send, p_recv.at[n], at(dx, NY - g, False, 0)).start()
    other[1, 0] = whole[1, 0]
    await_bytes(other.at[0], p_recv.at[0])
    await_bytes(other.at[1, pl.ds(1, 3)], p_recv.at[1])
    most = [jnp.maximum(other[0, g], other[1, g]) for g in range(NY)]
    for q, row in enumerate(turn(most)):
        turned[q] = row

    def give(b, carry):
        remote(turned.at[b // SUB], back.at[b], b_send, b_recv, at(0, 0, False, NZ - way(b))).start()
        return carry

    lax.fori_loop(0, NZ - 1, give, 0)
    back[NZ - 1] = turned[SUBS - 1]

    for g in ORDER[1:]:
        along_y[g].wait_send()
    for copy in shared:
        copy.wait_send()
    await_bytes(rank_mid.at[pl.ds(1, NY - 1)], yr_send)
    await_bytes(rank_got.at[pl.ds(0, NZ - 1)], zr_send)
    await_bytes(got.at[:, pl.ds(0, NZ - 1)], z_send)
    for j in range(4):
        await_bytes(got, x_send.at[j])
    for copy in halves:
        copy.wait_send()
    await_bytes(back.at[pl.ds(0, 7)], p_send)

    await_bytes(back.at[pl.ds(0, NZ - 1)], b_recv)
    total = jnp.zeros((1, ROWS), F32)
    for g, held in enumerate(collect(back)):
        one = held.astype(BF16).astype(F32)
        two = (held - one).astype(BF16).astype(F32)
        three = held - one - two
        row = iota((16, BIG), 0)
        split = jnp.where(row == 0, one, jnp.where(row == 1, two, jnp.where(row == 2, three, 0.0))).astype(BF16)
        picked = jnp.dot(split, place[g * BIG:(g + 1) * BIG, :], preferred_element_type=F32)
        total = total + (picked[0:1] + picked[1:2] + picked[2:3])
    out_ref[...] = total
    await_bytes(back.at[pl.ds(0, NZ - 1)], b_send)


def local(embeddings, cluster_ids, order_keys):
    dma = pltpu.SemaphoreType.DMA
    vmem = pltpu.VMEM
    out = pl.pallas_call(
        kernel,
        out_shape=jax.ShapeDtypeStruct((1, ROWS), F32),
        in_specs=[pl.BlockSpec(memory_space=pl.ANY)] * 3,
        out_specs=pl.BlockSpec(memory_space=vmem),
        scratch_shapes=[
            vmem((ROWS, D), BF16),
            vmem((1, ROWS), jnp.int32),
            vmem((1, ROWS), jnp.int32),
            vmem((NY * BIG, ROWS), BF16),
            vmem((NY, NZ, 16, D // 2), BF16),
            vmem((NY, NZ, 16, D // 2), BF16),
            vmem((NY, NZ, 16, D // 2), BF16),
            vmem((NY, 1, BIG), F32),
            vmem((NY, 1, BIG), F32),
            vmem((SUBS, 1, BIG), F32),
            vmem((NZ, 1, BIG), F32),
            vmem((5, NY, 1, BIG), F32),
            vmem((3, 5, BIG, D), BF16),
            vmem((2, 5, SMALL, D), BF16),
            vmem((4, 3, BIG, BIG), F32),
            vmem((16, 1, BIG), F32),
            vmem((16, 8, BIG), F32),
            vmem((4, NY, 1, BIG), F32),
            vmem((2, NY, 1, BIG), F32),
            vmem((2, NY, 1, BIG), F32),
            vmem((2, NY, 1, BIG), F32),
            vmem((SUBS, 1, BIG), F32),
            vmem((NZ, 1, BIG), F32),
            dma((3,)), dma((NY,)), dma((NY,)), dma, dma, dma, dma((NY, SUBS)), dma, dma,
            dma((4,)), dma((4 * SUBS, 4)), dma((4,)), dma((4,)), dma((2,)), dma((2,)), dma, dma((2,)), dma, dma,
        ],
        compiler_params=pltpu.CompilerParams(collective_id=0, has_side_effects=True, vmem_limit_bytes=56 * 2**20),
    )(embeddings, cluster_ids.reshape(1, ROWS), order_keys.reshape(1, ROWS))
    return out.reshape(ROWS)


def solution(mesh):
    placed = (P(("shard", "slot"), None), P(("shard", "slot")), P(("shard", "slot")))
    return jax.shard_map(local, mesh=mesh, in_specs=placed, out_specs=P(("shard", "slot")), check_vma=False)
```

time: 246 us -> 80.4 us (0.33)
  waiting for transfers between devices: 87.8 us -> 0 us
  Pallas kernels: 0 us -> 79.1 us
  blocking collectives: 76.8 us -> 0 us
  matrix products: 32.9 us -> 0 us
  starting transfers between devices: 15.5 us -> 0 us
  between operations: 13.5 us -> 0.02 us
  other arithmetic: 8.96 us -> 0 us
  local copies, waits for them, and re-layouts: 9.41 us -> 1.22 us
    pallas_call x0 -> x1, Pallas kernels: none -> 79.1 us  [local(): pl.pallas_call(kernel, out_shape=jax.ShapeDtypeStruct((1, ROWS), F32), in...]
    all_gather x1 -> x0, waiting for transfers between devices: 76.2 us -> none  [local(): key_rows = lax.all_gather(held_rows, 'slot', axis=0, tiled=True)]
    all_gather x2 -> x0, blocking collectives: 52.3 us -> none  [the longest x1 29.9 us: local(): key_cl = lax.all_gather(held_cl, 'slot', axis=0, tiled=True)]
    dot_general x16 -> x0, matrix products: 32.9 us -> none  [gram(): lax.dot_general(left, right, (((1,), (1,)), ((), ())), preferred_element_...]
    all_to_all x1 -> x0, blocking collectives: 24.5 us -> none  [local(): lax.all_to_all(send_rows, 'shard', split_axis=0, concat_axis=0, tiled=True)]
    all_to_all x3 -> x0, starting transfers between devices: 15.5 us -> none  [the longest x1 7.54 us: local(): lax.all_to_all(best, 'shard', split_axis=0, concat_axis=0, tiled=True)]
    all_to_all x3 -> x0, waiting for transfers between devices: 11.6 us -> none  [the longest x1 6.93 us: local(): lax.all_to_all(best, 'shard', split_axis=0, concat_axis=0, tiled=True)]
    all_to_all x8 -> x0, local copies, waits for them, and re-layouts: 3.29 us -> none  [the longest x3 1.27 us: local(): lax.all_to_all(best, 'shard', split_axis=0, concat_axis=0, tiled=True)]
  transfers between devices with their start and end apart: 4 -> 0, of which waited for: 3 -> 0; matrix products, arithmetic and copies ran while one was open for 2% -> 0% of each run, Pallas kernels for 0% -> 0%
where the time goes in v2:
time: 80.4 us; the launch traced here: 80.3 us
  Pallas kernels  79.1 us (98%)
  local copies, waits for them, and re-layouts  1.22 us (2%)
    pallas_call x1, Pallas kernels, local(): pl.pallas_call(kernel, out_shape=jax.ShapeDtypeStruct((1, ROWS), F32), in...  79.1 us

profile of v2, /device:TPU:1, one launch (start us, length us, event | category | flops | bytes accessed | tf_op | source)
XLA Modules:
  0.0 80.3 jit_solution(14687009556265118343)
XLA Ops:
  0.0 79.1 %shard_map.37 = f32[1,256]{1,0:T(1,128)} custom-call(bf16[256,768]{1,0:T(8,128)(2,1)} %x_hbm.1, s32[1,256]{1,0:T(1,128)} %bitcast.4, s32[1,256]{1,0:T(1,128)} %bitcast.5), custom_call_target="tpu_custom_call" | custom-call | tf_op jit(solution)/shard_map/pallas_call | solution.py:342
  79.1 0.0 copy-start
  79.1 0.7 copy-done
  79.7 0.6 copy.5
Async XLA Ops:
  79.1 0.7 copy-start

commit v3 on v2

--- a/solution.py
+++ b/solution.py
@@ -14,6 +14,7 @@
 SUB = 4
 SUBS = NZ // SUB
 PLACES = SUB * CAP
+AHEAD = 6
 LAG = 2
 NEVER = 1e9
 ORDER = (0, 1, 3, 2)
@@ -24,8 +25,7 @@
     return lax.broadcasted_iota(jnp.int32, shape, axis)
 
 
-def way(b):
-    return 8 + b // 2 - (b % 2) * (1 + 2 * (b // 2))
+WAY = (1, 15, 2, 14, 3, 13, 4, 12, 5, 11, 6, 10, 7, 9, 8, 0)
 
 
 def turn(rows):
@@ -48,7 +48,7 @@
 
 def kernel(x_hbm, ids_hbm, keys_hbm, out_ref, x_ref, ids_ref, keys_ref, place, sent, stage, got, rank_out, rank_mid,
            rank_turned, rank_got, ranks, big, small, keyed, query, best, part, half, whole, other, turned, back,
-           in_sem, y_send, y_recv, yr_send, yr_recv, z_send, z_recv, zr_send, zr_recv, x_send, x_recv, xr_send, xr_recv,
+           in_sem, ready, y_send, y_recv, yr_send, yr_recv, z_send, z_recv, zr_send, zr_recv, x_send, x_recv, xr_send, xr_recv,
            h_send, h_recv, p_send, p_recv, b_send, b_recv):
     shard, z = lax.axis_index("shard"), lax.axis_index("slot")
     x, y, core = shard // 8, (shard // 2) % 4, shard % 2
@@ -80,13 +80,12 @@
         greet(at(0, 0, False, d))
         return carry
 
-    for device in (twin, right):
+    above, below = at(0, 0, False, 1), at(0, 0, False, 15)
+    for device in (twin, right, left, above, below):
         greet(device)
-    for g in range(NY):
+    for g in range(1, NY):
         greet(at(3, g, False, 0))
-        if g:
-            greet(at(0, g, False, 0))
-    lax.fori_loop(1, NZ, greet_z, 0)
+        greet(at(0, g, False, 0))
 
     loads[0].wait()
     ids = ids_ref[...]
@@ -94,7 +93,9 @@
     before = (across == jnp.transpose(across)) & (iota((ROWS, ROWS), 0) < iota((ROWS, ROWS), 1))
     position = jnp.sum(jnp.where(before, 1.0, 0.0), axis=0, keepdims=True).astype(jnp.int32)
     step_y, step_z = ((ids & 3) + NY - y) & (NY - 1), ((ids >> 2) + NZ - z) & (NZ - 1)
-    block = jnp.where(step_z < 8, 15 - 2 * step_z, 2 * step_z - 16)
+    block = jnp.zeros_like(ids)
+    for b in range(NZ):
+        block = jnp.where(step_z == WAY[b], b, block)
     target = (step_y * NZ + block) * CAP + position
     place[...] = jnp.where(iota((NY * BIG, ROWS), 0) == target, 1.0, 0.0).astype(BF16)
 
@@ -116,46 +117,62 @@
         halves = [laid[:, :D // 2].reshape(NZ, CAP, D // 2), laid[:, D // 2:].reshape(NZ, CAP, D // 2)]
         sent[g] = jnp.concatenate(halves, axis=1).astype(BF16)
 
-    pl.semaphore_wait(barrier, 24)
-
-    def along_z(g, source):
-        def go(b, carry):
-            remote(source.at[g, b], got.at[g, b], z_send, z_recv.at[g, b // SUB], at(0, 0, False, way(b))).start()
-            return carry
-
-        lax.fori_loop(0, NZ - 1, go, 0)
-        got[g, NZ - 1] = source[g, NZ - 1]
+    pl.semaphore_wait(barrier, 11)
+
+    def tell(d):
+        pl.semaphore_signal(ready.at[0, d], inc=1, device_id=below, device_id_type=MESH)
+        if d < NZ // 2:
+            pl.semaphore_signal(ready.at[1, d], inc=1, device_id=above, device_id_type=MESH)
+
+    def hear(d):
+        pl.semaphore_wait(ready.at[0, d], 1)
+        if d < NZ // 2:
+            pl.semaphore_wait(ready.at[1, d], 1)
+            tell(d + 1)
+
+    tell(2)
+
+    def along_z(n):
+        i, sub = divmod(n, SUBS)
+        g, source = ORDER[i], stage if i else sent
+        if i and sub == 0:
+            along_y[g].wait_recv()
+        for b in range(sub * SUB, (sub + 1) * SUB):
+            if i == 0 and b % 2 == 0 and b >= 2:
+                hear(WAY[b])
+            if WAY[b]:
+                remote(source.at[g, b], got.at[g, b], z_send, z_recv.at[g, sub], at(0, 0, False, WAY[b])).start()
+            else:
+                got[g, b] = source[g, b]
 
     for g in ORDER[1:]:
         remote(rank_out.at[g], rank_mid.at[g], yr_send, yr_recv, at(0, g, False, 0)).start()
     along_y = {g: remote(sent.at[g], stage.at[g], y_send.at[g], y_recv.at[g], at(0, g, False, 0)) for g in ORDER[1:]}
-    along_y[1].start()
-    along_z(0, sent)
-    along_y[3].start()
-    along_y[2].start()
+    for g in ORDER[1:]:
+        along_y[g].start()
+    for n in range(SUBS):
+        along_z(n)
 
     best[...] = jnp.full(best.shape, -1.0, F32)
     await_bytes(rank_mid.at[pl.ds(1, NY - 1)], yr_recv)
     for q, row in enumerate(turn([rank_out[0]] + [rank_mid[g] for g in range(1, NY)])):
         rank_turned[q] = row
 
-    def ranks_along_z(b, carry):
-        remote(rank_turned.at[b // SUB], rank_got.at[b], zr_send, zr_recv, at(0, 0, False, way(b))).start()
-        return carry
-
-    lax.fori_loop(0, NZ - 1, ranks_along_z, 0)
+    for b in range(NZ - 1):
+        remote(rank_turned.at[b // SUB], rank_got.at[b], zr_send, zr_recv, at(0, 0, False, WAY[b])).start()
     rank_got[NZ - 1] = rank_turned[SUBS - 1]
-    for g in ORDER[1:]:
-        along_y[g].wait_recv()
-        along_z(g, stage)
-
-    await_bytes(rank_got.at[pl.ds(0, NZ - 1)], zr_recv)
-    for g, row in enumerate(collect(rank_got)):
-        ranks[A0, g] = row
+    for n in range(SUBS, AHEAD):
+        along_z(n)
+
     shared = [remote(ranks.at[a], ranks.at[b], xr_send.at[i], xr_recv.at[i], device)
               for i, (a, b, device) in enumerate(((A0, R0, left), (A0, L0, right), (A0, A1, twin), (R0, R1, twin)))]
-    for copy in shared[:3]:
-        copy.start()
+
+    def gather_ranks():
+        await_bytes(rank_got.at[pl.ds(0, NZ - 1)], zr_recv)
+        for g, row in enumerate(collect(rank_got)):
+            ranks[A0, g] = row
+        for copy in shared[:3]:
+            copy.start()
 
     def rows_of(i, sub, a):
         if i < 3:
@@ -262,7 +279,11 @@
 
     for n in range(4 * SUBS):
         pass_on(n // SUBS, n % SUBS)
-        if n == 0:
+        if n + AHEAD < 4 * SUBS:
+            along_z(n + AHEAD)
+        if n == 1:
+            gather_ranks()
+        if n == SUBS:
             learn_ranks()
         if n >= LAG:
             pass_twin((n - LAG) // SUBS, (n - LAG) % SUBS)
@@ -302,11 +323,8 @@
     for q, row in enumerate(turn(most)):
         turned[q] = row
 
-    def give(b, carry):
-        remote(turned.at[b // SUB], back.at[b], b_send, b_recv, at(0, 0, False, NZ - way(b))).start()
-        return carry
-
-    lax.fori_loop(0, NZ - 1, give, 0)
+    for b in range(NZ - 1):
+        remote(turned.at[b // SUB], back.at[b], b_send, b_recv, at(0, 0, False, NZ - WAY[b])).start()
     back[NZ - 1] = turned[SUBS - 1]
 
     for g in ORDER[1:]:
@@ -368,7 +386,7 @@
             vmem((2, NY, 1, BIG), F32),
             vmem((SUBS, 1, BIG), F32),
             vmem((NZ, 1, BIG), F32),
-            dma((3,)), dma((NY,)), dma((NY,)), dma, dma, dma, dma((NY, SUBS)), dma, dma,
+            dma((3,)), pltpu.SemaphoreType.REGULAR((2, NZ // 2 + 1)), dma((NY,)), dma((NY,)), dma, dma, dma, dma((NY, SUBS)), dma, dma,
             dma((4,)), dma((4 * SUBS, 4)), dma((4,)), dma((4,)), dma((2,)), dma((2,)), dma, dma((2,)), dma, dma,
         ],
         compiler_params=pltpu.CompilerParams(collective_id=0, has_side_effects=True, vmem_limit_bytes=56 * 2**20),

time: 80.4 us -> 77.3 us (0.961)
  Pallas kernels: 79.1 us -> 75.9 us
    pallas_call x1, Pallas kernels: 79.1 us -> 75.9 us  [local(): pl.pallas_call(kernel, out_shape=jax.ShapeDtypeStruct((1, ROWS), F32), in...]
where the time goes in v3:
time: 77.3 us; the launch traced here: 77.1 us
  Pallas kernels  75.9 us (98%)
  local copies, waits for them, and re-layouts  1.22 us (2%)
    pallas_call x1, Pallas kernels, local(): pl.pallas_call(kernel, out_shape=jax.ShapeDtypeStruct((1, ROWS), F32), in...  75.9 us

profile of v3, /device:TPU:1, one launch (start us, length us, event | category | flops | bytes accessed | tf_op | source)
XLA Modules:
  0.0 77.1 jit_solution(15161909206818357546)
XLA Ops:
  0.0 75.9 %shard_map.37 = f32[1,256]{1,0:T(1,128)} custom-call(bf16[256,768]{1,0:T(8,128)(2,1)} %x_hbm.1, s32[1,256]{1,0:T(1,128)} %bitcast.4, s32[1,256]{1,0:T(1,128)} %bitcast.5), custom_call_target="tpu_custom_call" | custom-call | tf_op jit(solution)/shard_map/pallas_call | solution.py:360
  75.9 0.0 copy-start
  75.9 0.7 copy-done
  76.6 0.6 copy.5
Async XLA Ops:
  75.9 0.7 copy-start

commit v4 on v3

--- a/solution.py
+++ b/solution.py
@@ -18,7 +18,8 @@
 LAG = 2
 NEVER = 1e9
 ORDER = (0, 1, 3, 2)
-A1, A0, R0, R1, L0 = range(5)
+A1, A0, L0, R0, R1 = range(5)
+KEYS, QUERIES = (A0, L0, R0), (A1, A0, R0, R1)
 
 
 def iota(shape, axis):
@@ -158,7 +159,7 @@
     for q, row in enumerate(turn([rank_out[0]] + [rank_mid[g] for g in range(1, NY)])):
         rank_turned[q] = row
 
-    for b in range(NZ - 1):
+    for b in reversed(range(NZ - 1)):
         remote(rank_turned.at[b // SUB], rank_got.at[b], zr_send, zr_recv, at(0, 0, False, WAY[b])).start()
     rank_got[NZ - 1] = rank_turned[SUBS - 1]
     for n in range(SUBS, AHEAD):
@@ -203,14 +204,14 @@
             copy.wait_recv()
         shared[3].start()
         for i, g in enumerate(ORDER):
-            for s, a in enumerate((A0, R0, L0)):
+            for s, a in enumerate(KEYS):
                 rank = ranks[a, g]
                 rank = jnp.where(rank > 0.5, rank, NEVER)
                 keyed[i, s] = jnp.transpose(jnp.broadcast_to(rank, (BIG, BIG)))
         shared[3].wait_recv()
         for i in range(3):
-            for a in (A1, A0, R0, R1):
-                query[4 * i + a] = ranks[a, ORDER[i]]
+            for j, a in enumerate(QUERIES):
+                query[4 * i + j] = ranks[a, ORDER[i]]
         low = iota((1, BIG), 1) < SMALL
         for s, (a, b) in enumerate(((A1, A0), (R0, R1))):
             one, two = ranks[a, ORDER[3]], ranks[b, ORDER[3]]
@@ -221,43 +222,40 @@
         return lax.dot_general(k, q, (((1,), (1,)), ((), ())), preferred_element_type=F32)
 
     def rows_in(p, a, b):
-        if isinstance(p, int) and p >= 3:
+        if p >= 3:
             return small[p - 3, a:b].reshape((b - a) * SMALL, D)
         return big[p, a:b].reshape((b - a) * BIG, D)
 
     def key_ranks(p, s):
-        if isinstance(p, int) and p >= 3:
+        if p >= 3:
             return keyed[3, s, (p - 3) * SMALL:(p - 2) * SMALL]
         return keyed[p, s]
 
-    def groups(q, outer):
-        if isinstance(q, int) and q >= 3:
-            return [12 + 2 * (q - 3) + s for s in range(2 if outer else 1)]
-        return [4 * q + a for a in range(4 if outer else 2)]
+    def groups(q, far):
+        if q >= 3:
+            return [12 + 2 * (q - 3) + far]
+        return [4 * q + 2 * far, 4 * q + 2 * far + 1]
 
     def fold(sims, rank, j):
         masked = jnp.where(rank < query[j], sims, -1.0)
         best[j] = jnp.maximum(best[j], jnp.max(masked.reshape(sims.shape[0] // 8, 8, 128), axis=0))
 
     def inner(k, q):
-        sims = dots(rows_in(k, A0, R1), rows_in(q, A1, R0))
-        size = sims.shape[0] // 2
-        for s in range(2):
-            for n, j in enumerate(groups(q, False)):
+        sims = dots(rows_in(k, A0, R1), rows_in(q, A1, L0))
+        size = sims.shape[0] // 3
+        for s in range(3):
+            for n, j in enumerate(groups(q, 0)):
                 fold(sims[s * size:(s + 1) * size, n * 128:(n + 1) * 128], key_ranks(k, s), j)
 
     def outer(k, q):
-        sims = dots(rows_in(k, L0, L0 + 1), rows_in(q, A1, L0))
-        for n, j in enumerate(groups(q, True)):
-            fold(sims[:, n * 128:(n + 1) * 128], key_ranks(k, 2), j)
+        sims = dots(rows_in(k, L0, R0), rows_in(q, R0, R1 + 1))
+        for n, j in enumerate(groups(q, 1)):
+            fold(sims[:, n * 128:(n + 1) * 128], key_ranks(k, 1), j)
 
     def pairs(p, work):
-        def one(h, carry):
+        for h in range(min(p, 3)):
             work(h, p)
             work(p, h)
-            return carry
-
-        lax.fori_loop(0, min(p, 3), one, 0)
         if p == 4:
             work(3, 4)
             work(4, 3)
@@ -269,11 +267,11 @@
     def compare_inner(p):
         for i, sub in subs_of(p):
             passed(i, sub, 2).wait_recv()
+            passed(i, sub, 1).wait_recv()
         pairs(p, inner)
 
     def compare_outer(p):
         for i, sub in subs_of(p):
-            passed(i, sub, 1).wait_recv()
             passed(i, sub, 3).wait_recv()
         pairs(p, outer)
 
@@ -301,10 +299,10 @@
 
     low = iota((1, BIG), 1) < SMALL
     top = [jnp.max(best[j], axis=0, keepdims=True) for j in range(16)]
-    for a in (A1, A0, R0, R1):
+    for j, a in enumerate(QUERIES):
         for i in range(3):
-            part[a, ORDER[i]] = top[4 * i + a]
-        one, two = top[12 + a // 2], top[14 + a // 2]
+            part[a, ORDER[i]] = top[4 * i + j]
+        one, two = top[12 + j // 2], top[14 + j // 2]
         part[a, ORDER[3]] = (jnp.where(low, one, pltpu.roll(two, SMALL, 1)) if a in (A1, R0) else
                              jnp.where(low, pltpu.roll(one, SMALL, 1), two))
     halves = [remote(part.at[a], half.at[i], h_send.at[i], h_recv.at[i], twin) for i, a in enumerate((R1, A1))]
@@ -323,7 +321,7 @@
     for q, row in enumerate(turn(most)):
         turned[q] = row
 
-    for b in range(NZ - 1):
+    for b in reversed(range(NZ - 1)):
         remote(turned.at[b // SUB], back.at[b], b_send, b_recv, at(0, 0, False, NZ - WAY[b])).start()
     back[NZ - 1] = turned[SUBS - 1]
 
@@ -350,7 +348,7 @@
         split = jnp.where(row == 0, one, jnp.where(row == 1, two, jnp.where(row == 2, three, 0.0))).astype(BF16)
         picked = jnp.dot(split, place[g * BIG:(g + 1) * BIG, :], preferred_element_type=F32)
         total = total + (picked[0:1] + picked[1:2] + picked[2:3])
-    out_ref[...] = total
+    out_ref[...] = total.reshape(ROWS)
     await_bytes(back.at[pl.ds(0, NZ - 1)], b_send)
 
 
@@ -359,7 +357,7 @@
     vmem = pltpu.VMEM
     out = pl.pallas_call(
         kernel,
-        out_shape=jax.ShapeDtypeStruct((1, ROWS), F32),
+        out_shape=jax.ShapeDtypeStruct((ROWS,), F32),
         in_specs=[pl.BlockSpec(memory_space=pl.ANY)] * 3,
         out_specs=pl.BlockSpec(memory_space=vmem),
         scratch_shapes=[
@@ -380,7 +378,7 @@
             vmem((4, 3, BIG, BIG), F32),
             vmem((16, 1, BIG), F32),
             vmem((16, 8, BIG), F32),
-            vmem((4, NY, 1, BIG), F32),
+            vmem((5, NY, 1, BIG), F32),
             vmem((2, NY, 1, BIG), F32),
             vmem((2, NY, 1, BIG), F32),
             vmem((2, NY, 1, BIG), F32),
@@ -391,7 +389,7 @@
         ],
         compiler_params=pltpu.CompilerParams(collective_id=0, has_side_effects=True, vmem_limit_bytes=56 * 2**20),
     )(embeddings, cluster_ids.reshape(1, ROWS), order_keys.reshape(1, ROWS))
-    return out.reshape(ROWS)
+    return out
 
 
 def solution(mesh):

time: 77.3 us -> 75.8 us (0.981)
  Pallas kernels: 75.9 us -> 74.4 us
    pallas_call x1, Pallas kernels: 75.9 us -> 74.4 us  [local(): pl.pallas_call(kernel, out_shape=jax.ShapeDtypeStruct((ROWS,), F32), in_s...]
where the time goes in v4:
time: 75.8 us; the launch traced here: 75.6 us
  Pallas kernels  74.4 us (98%)
  local copies, waits for them, and re-layouts  1.24 us (2%)
    pallas_call x1, Pallas kernels, local(): pl.pallas_call(kernel, out_shape=jax.ShapeDtypeStruct((ROWS,), F32), in_s...  74.4 us

profile of v4, /device:TPU:1, one launch (start us, length us, event | category | flops | bytes accessed | tf_op | source)
XLA Modules:
  0.0 75.6 jit_solution(4724982008410272415)
XLA Ops:
  0.0 74.4 %shard_map.37 = f32[256]{0:T(256)} custom-call(bf16[256,768]{1,0:T(8,128)(2,1)} %x_hbm.1, s32[1,256]{1,0:T(1,128)} %bitcast.2, s32[1,256]{1,0:T(1,128)} %bitcast.3), custom_call_target="tpu_custom_call" | custom-call | tf_op jit(solution)/shard_map/pallas_call | solution.py:358
  74.4 1.2 %copy.5 = f32[256]{0:T(256)} copy(f32[256]{0:T(256)} %shard_map.37) | data formatting | bytes 2048

commit v5 on v4

--- a/solution.py
+++ b/solution.py
@@ -247,6 +247,18 @@
             for n, j in enumerate(groups(q, 0)):
                 fold(sims[s * size:(s + 1) * size, n * 128:(n + 1) * 128], key_ranks(k, s), j)
 
+    def own(k, q):
+        sims = dots(rows_in(k, A0, L0), rows_in(q, A1, L0))
+        for n, j in enumerate(groups(q, 0)):
+            fold(sims[:, n * 128:(n + 1) * 128], key_ranks(k, 0), j)
+
+    def beside(k, q):
+        sims = dots(rows_in(k, L0, R1), rows_in(q, A1, L0))
+        size = sims.shape[0] // 2
+        for s in range(2):
+            for n, j in enumerate(groups(q, 0)):
+                fold(sims[s * size:(s + 1) * size, n * 128:(n + 1) * 128], key_ranks(k, 1 + s), j)
+
     def outer(k, q):
         sims = dots(rows_in(k, L0, R0), rows_in(q, R0, R1 + 1))
         for n, j in enumerate(groups(q, 1)):
@@ -292,22 +304,32 @@
             compare_outer(i - 1)
     compare_inner(3)
     compare_outer(3)
-    for n in range(4 * SUBS - LAG, 4 * SUBS):
-        pass_twin(n // SUBS, n % SUBS)
-    compare_inner(4)
+    pass_twin(3, 2)
+    for i, sub in subs_of(4):
+        passed(i, sub, 2).wait_recv()
+    pairs(4, own)
+    pass_twin(3, 3)
+    for i, sub in subs_of(4):
+        passed(i, sub, 1).wait_recv()
+    pairs(4, beside)
+
+    low = iota((1, BIG), 1) < SMALL
+
+    def gather_top(one_set):
+        for j in (2 * one_set, 2 * one_set + 1):
+            a = QUERIES[j]
+            for i in range(3):
+                part[a, ORDER[i]] = jnp.max(best[4 * i + j], axis=0, keepdims=True)
+            one, two = [jnp.max(best[m + one_set], axis=0, keepdims=True) for m in (12, 14)]
+            part[a, ORDER[3]] = (jnp.where(low, one, pltpu.roll(two, SMALL, 1)) if a in (A1, R0) else
+                                 jnp.where(low, pltpu.roll(one, SMALL, 1), two))
+
+    halves = [remote(part.at[a], half.at[i], h_send.at[i], h_recv.at[i], twin) for i, a in enumerate((R1, A1))]
+    gather_top(0)
+    halves[1].start()
     compare_outer(4)
-
-    low = iota((1, BIG), 1) < SMALL
-    top = [jnp.max(best[j], axis=0, keepdims=True) for j in range(16)]
-    for j, a in enumerate(QUERIES):
-        for i in range(3):
-            part[a, ORDER[i]] = top[4 * i + j]
-        one, two = top[12 + j // 2], top[14 + j // 2]
-        part[a, ORDER[3]] = (jnp.where(low, one, pltpu.roll(two, SMALL, 1)) if a in (A1, R0) else
-                             jnp.where(low, pltpu.roll(one, SMALL, 1), two))
-    halves = [remote(part.at[a], half.at[i], h_send.at[i], h_recv.at[i], twin) for i, a in enumerate((R1, A1))]
-    for copy in halves:
-        copy.start()
+    gather_top(1)
+    halves[0].start()
     for n, (a, dx) in enumerate(((R0, 1), (A0, 0))):
         halves[n].wait_recv()
         for g in (2, 1, 3, 0):

time: 75.8 us -> 75.5 us (level)
  no operation moved by 1% of the time
where the time goes in v5:
time: 75.5 us; the launch traced here: 75.4 us
  Pallas kernels  74.1 us (98%)
  local copies, waits for them, and re-layouts  1.24 us (2%)
    pallas_call x1, Pallas kernels, local(): pl.pallas_call(kernel, out_shape=jax.ShapeDtypeStruct((ROWS,), F32), in_s...  74.1 us

profile of v5, /device:TPU:1, one launch (start us, length us, event | category | flops | bytes accessed | tf_op | source)
XLA Modules:
  0.0 75.4 jit_solution(1291055819216460722)
XLA Ops:
  0.0 74.1 %shard_map.37 = f32[256]{0:T(256)} custom-call(bf16[256,768]{1,0:T(8,128)(2,1)} %x_hbm.1, s32[1,256]{1,0:T(1,128)} %bitcast.2, s32[1,256]{1,0:T(1,128)} %bitcast.3), custom_call_target="tpu_custom_call" | custom-call | tf_op jit(solution)/shard_map/pallas_call | solution.py:380
  74.1 1.2 %copy.5 = f32[256]{0:T(256)} copy(f32[256]{0:T(256)} %shard_map.37) | data formatting | bytes 2048

commit v6 on v5

--- a/solution.py
+++ b/solution.py
@@ -14,7 +14,7 @@
 SUB = 4
 SUBS = NZ // SUB
 PLACES = SUB * CAP
-AHEAD = 6
+AHEAD = 7
 LAG = 2
 NEVER = 1e9
 ORDER = (0, 1, 3, 2)

time: 75.5 us -> 75.8 us (level)
  no operation moved by 1% of the time
where the time goes in v6:
time: 75.8 us; the launch traced here: 75.6 us
  Pallas kernels  74.4 us (98%)
  local copies, waits for them, and re-layouts  1.24 us (2%)
    pallas_call x1, Pallas kernels, local(): pl.pallas_call(kernel, out_shape=jax.ShapeDtypeStruct((ROWS,), F32), in_s...  74.4 us

profile of v6, /device:TPU:1, one launch (start us, length us, event | category | flops | bytes accessed | tf_op | source)
XLA Modules:
  0.0 75.6 jit_solution(4336814837883336168)
XLA Ops:
  0.0 74.4 %shard_map.37 = f32[256]{0:T(256)} custom-call(bf16[256,768]{1,0:T(8,128)(2,1)} %x_hbm.1, s32[1,256]{1,0:T(1,128)} %bitcast.2, s32[1,256]{1,0:T(1,128)} %bitcast.3), custom_call_target="tpu_custom_call" | custom-call | tf_op jit(solution)/shard_map/pallas_call | solution.py:380
  74.4 1.2 %copy.5 = f32[256]{0:T(256)} copy(f32[256]{0:T(256)} %shard_map.37) | data formatting | bytes 2048
